TPU v7x, 32 devices: a whole 2x2x4 slice. The times are simulated.
32 devices in a mesh: ex: 4 (over x, core), ft: 8 (over z, y).
Axes of the slice: x: 2, y: 2, z: 4, core: 2. Of those that a mesh axis runs over, the one named last changes fastest.
Arguments:
- features: bfloat16 [32768, 16384], P('ex', 'ft'), as said below
- targets: float32 [8, 32768], P(None, 'ex'), may hold values from -36 to 36, as said below
Outputs:
- estimate: float32 [8, 16384], P(None, 'ft')
- misfit: float32 [8, 32768], P(None, 'ex')
Inputs may be any that keep to these rules, and one draw needn't show every extreme that they name: Finite; row and column scales vary over examples and features. `targets`: Finite.
All inputs are finite; a program needn't handle non-finite values.
Results may differ from a plain program's by a relative error of at most 0.0034.
Values sent between devices are 32-bit elements; how exact they have to be, the bound alone decides.
A program may use at most 64 MiB of HBM per device.

v0:
```python
import jax
import jax.numpy as jnp
from jax import lax
from jax.sharding import PartitionSpec as P

ITERS = 2


eps = 1e-06


def row_step(features, right_vec, alpha_norm, left_old):
    partial_value = lax.dot_general(
        right_vec.astype(jnp.bfloat16),
        features,
        (((1,), (1,)), ((), ())),
        preferred_element_type=jnp.float32,
    )
    summed = lax.psum(partial_value, "ft")
    fresh = summed - alpha_norm * left_old
    square = lax.psum(jnp.sum(fresh * fresh, axis=1, keepdims=True), "ex")
    beta_norm = jnp.sqrt(square + eps)
    return (fresh / beta_norm, beta_norm)


def column_step(features, left_vec, beta_norm, right_old):
    partial_value = jnp.dot(
        left_vec.astype(jnp.bfloat16), features, preferred_element_type=jnp.float32
    )
    summed = lax.psum(partial_value, "ex")
    fresh = summed - beta_norm * right_old
    square = lax.psum(jnp.sum(fresh * fresh, axis=1, keepdims=True), "ft")
    alpha_norm = jnp.sqrt(square + eps)
    return (fresh / alpha_norm, alpha_norm)


def shards(features, targets):
    start_sq = lax.psum(jnp.sum(targets * targets, axis=1, keepdims=True), "ex")
    beta_norm = jnp.sqrt(start_sq + eps)
    left_vec = targets / beta_norm
    empty = jnp.zeros((targets.shape[0], features.shape[1]), jnp.float32)
    right_vec, alpha_norm = column_step(features, left_vec, jnp.zeros_like(beta_norm), empty)
    search = right_vec
    estimate = empty
    phi_bar = beta_norm
    rho_bar = alpha_norm
    for step in range(ITERS):
        left_vec, beta_norm = row_step(features, right_vec, alpha_norm, left_vec)
        right_vec, alpha_norm = column_step(features, left_vec, beta_norm, right_vec)
        rho_value = jnp.sqrt(rho_bar * rho_bar + beta_norm * beta_norm)
        cosine = rho_bar / rho_value
        sine_value = beta_norm / rho_value
        theta_value = sine_value * alpha_norm
        rho_bar = -cosine * alpha_norm
        phi_value = cosine * phi_bar
        phi_bar = sine_value * phi_bar
        estimate = estimate + phi_value / rho_value * search
        search = right_vec - theta_value / rho_value * search
    fitted = lax.dot_general(
        estimate.astype(jnp.bfloat16),
        features,
        (((1,), (1,)), ((), ())),
        preferred_element_type=jnp.float32,
    )
    fitted = lax.psum(fitted, "ft")
    return (estimate, targets - fitted)


def solution(mesh):
    placed = (P("ex", "ft"), P(None, "ex"))
    return jax.shard_map(
        shards,
        mesh=mesh,
        in_specs=placed,
        out_specs=(P(None, "ft"), P(None, "ex")),
        check_vma=False,
    )
```

profile of v0, /device:TPU:0, one launch (start us, length us, event | category | flops | bytes accessed | tf_op | source)
XLA Modules:
  0.0 427.6 jit_solution(11514942095769818863)
XLA Ops:
  7.2 0.0 all-reduce.6.cloned.1.call-start
  7.2 1.1 multiply_reduce_fusion.2
  8.3 8.3 %psum.70 = f32[8,1]{0,1:T(1,128)S(1)} all-reduce(f32[8,1]{0,1:T(1,128)S(1)} %bitcast.25), channel_id=1, replica_groups=mesh['ex'=4,'ft'=8] {'ex'}, use_global_device_ids=true, to_apply=%region_1.0 | all-reduce | flops 8 | bytes 64 | tf_op jit(solution)/shard_map/psum | solution.py:38
  16.7 0.0 copy-start
  16.7 15.8 %fusion.2 = f32[8,2048]{1,0:T(8,128)} fusion(bf16[8192,2048]{1,0:T(8,128)(2,1)} %param.2, f32[8,8192]{1,0:T(8,128)} %param.3, f32[8]{0:T(128)S(1)} %fusion.13), kind=kOutput, calls=%fused_computation.7 | convolution fusion | flops 268566528 | bytes 33882144 | tf_op jit(solution)/shard_map/dot_general | solution.py:27
  32.5 0.0 all-reduce.6.cloned.1.call-update
  32.5 0.0 all-reduce.8.cloned.1.call-start
  32.5 31.5 %all-reduce.6.cloned.1.call-done = f32[8,2048]{1,0:T(8,128)} async-done(((f32[8,2048]{1,0:T(8,128)}), f32[8,2048]{1,0:T(8,128)}) %all-reduce.6.cloned.1.call-update) | async-done | bytes 65552 | tf_op jit(solution)/shard_map/psum | solution.py:30
  64.0 1.0 multiply_reduce_fusion.4
  65.0 21.4 %psum.72 = f32[8,1]{0,1:T(1,128)S(1)} all-reduce(f32[8,1]{0,1:T(1,128)S(1)} %bitcast.26), channel_id=1, replica_groups=mesh['ex'=4,'ft'=8] {'ft'}, use_global_device_ids=true, to_apply=%region_4.0 | all-reduce | flops 8 | bytes 64 | tf_op jit(solution)/shard_map/psum | solution.py:32
  86.4 0.0 copy-start.1
  86.4 18.1 %fusion.8 = f32[8,8192]{1,0:T(8,128)} fusion(bf16[8192,2048]{1,0:T(8,128)(2,1)} %param.2, f32[8,2048]{1,0:T(8,128)} %all-reduce.6.cloned.1.call-done, f32[8]{0:T(128)S(1)} %fusion.15), kind=kOutput, calls=%fused_computation.19 | convolution fusion | flops 268468224 | bytes 33882144 | tf_op jit(solution)/shard_map/dot_general | solution.py:13
  104.4 0.0 all-reduce.8.cloned.1.call-update
  104.5 0.0 all-reduce.10.cloned.1.call-start
  104.5 66.9 %all-reduce.8.cloned.1.call-done = f32[8,8192]{1,0:T(8,128)} async-done(((f32[8,8192]{1,0:T(8,128)}), f32[8,8192]{1,0:T(8,128)}) %all-reduce.8.cloned.1.call-update) | async-done | bytes 262160 | tf_op jit(solution)/shard_map/psum | solution.py:19
  171.4 0.0 copy-done
  171.4 1.2 multiply_reduce_fusion.1
  172.6 5.7 %psum.74 = f32[8,1]{0,1:T(1,128)S(1)} all-reduce(f32[8,1]{0,1:T(1,128)S(1)} %bitcast.28), channel_id=1, replica_groups=mesh['ex'=4,'ft'=8] {'ex'}, use_global_device_ids=true, to_apply=%region_7.0 | all-reduce | flops 8 | bytes 64 | tf_op jit(solution)/shard_map/psum | solution.py:21
  178.3 13.5 %fusion = f32[8,2048]{1,0:T(8,128)} fusion(bf16[8192,2048]{1,0:T(8,128)(2,1)} %param.2, f32[8,8192]{1,0:T(8,128)S(1)} %get-tuple-element.8, f32[8]{0:T(128)S(1)} %get-tuple-element.9), kind=kOutput, calls=%fused_computation.4 | convolution fusion | flops 268566528 | bytes 33882144 | tf_op jit(solution)/shard_map/dot_general | solution.py:27
  191.8 0.0 all-reduce.10.cloned.1.call-update
  191.8 0.0 all-reduce.12.cloned.1.call-start
  191.9 30.7 %all-reduce.10.cloned.1.call-done = f32[8,2048]{1,0:T(8,128)} async-done(((f32[8,2048]{1,0:T(8,128)}), f32[8,2048]{1,0:T(8,128)}) %all-reduce.10.cloned.1.call-update) | async-done | bytes 65552 | tf_op jit(solution)/shard_map/psum | solution.py:30
  222.6 0.0 copy-done.1
  222.6 0.0 copy-start.2
  222.6 1.1 multiply_reduce_fusion.3
  223.7 21.5 %psum.76 = f32[8,1]{0,1:T(1,128)S(1)} all-reduce(f32[8,1]{0,1:T(1,128)S(1)} %bitcast.27), channel_id=1, replica_groups=mesh['ex'=4,'ft'=8] {'ft'}, use_global_device_ids=true, to_apply=%region_10.0 | all-reduce | flops 8 | bytes 64 | tf_op jit(solution)/shard_map/psum | solution.py:32
  245.2 15.2 %fusion.6 = f32[8,8192]{1,0:T(8,128)} fusion(bf16[8192,2048]{1,0:T(8,128)(2,1)} %param.2, f32[8]{0:T(128)S(1)} %fusion.18, f32[8,2048]{1,0:T(8,128)} %all-reduce.10.cloned.1.call-done, f32[8]{0:T(128)S(1)} %get-tuple-element.9, f32[8,2048]{1,0:T(8,128)S(1)} %copy-done.1, f32[8]{0:T(128)S(1)} %fusion.15), kind=kOutput, calls=%fused_computation.16 | convolution fusion | flops 268517376 | bytes 33947744 | tf_op jit(solution)/shard_map/dot_general | solution.py:13
  260.4 0.0 all-reduce.12.cloned.1.call-update
  260.4 0.0 all-reduce.14.cloned.1.call-start
  260.5 66.9 %all-reduce.12.cloned.1.call-done = f32[8,8192]{1,0:T(8,128)} async-done(((f32[8,8192]{1,0:T(8,128)}), f32[8,8192]{1,0:T(8,128)}) %all-reduce.12.cloned.1.call-update) | async-done | bytes 262160 | tf_op jit(solution)/shard_map/psum | solution.py:19
  327.4 1.2 multiply_reduce_fusion
  328.6 5.7 %psum.78 = f32[8,1]{0,1:T(1,128)S(1)} all-reduce(f32[8,1]{0,1:T(1,128)S(1)} %bitcast.24), channel_id=1, replica_groups=mesh['ex'=4,'ft'=8] {'ex'}, use_global_device_ids=true, to_apply=%region_13.0 | all-reduce | flops 8 | bytes 64 | tf_op jit(solution)/shard_map/psum | solution.py:21
  334.3 0.0 copy-done.2
  334.3 0.1 multiply_add_fusion
  334.4 0.0 copy-start.3
  334.4 14.7 %fusion.4 = f32[8,8192]{1,0:T(8,128)} fusion(bf16[8192,2048]{1,0:T(8,128)(2,1)} %param.2, f32[8,2048]{1,0:T(8,128)S(1)} %multiply_add_fusion), kind=kOutput, calls=%fused_computation.14 | convolution fusion | flops 268451840 | bytes 33882112 | tf_op jit(solution)/shard_map/dot_general | solution.py:59
  349.1 0.0 all-reduce.14.cloned.1.call-update
  349.1 70.3 %all-reduce.14.cloned.1.call-done = f32[8,8192]{1,0:T(8,128)} async-done(((f32[8,8192]{1,0:T(8,128)}), f32[8,8192]{1,0:T(8,128)}) %all-reduce.14.cloned.1.call-update) | async-done | bytes 262160 | tf_op jit(solution)/shard_map/psum | solution.py:65
  419.4 1.7 sub.19
  421.1 0.0 copy-done.3
  (6 shorter events, 0.1 us)
Async XLA Ops:
  7.2 56.9 %all-reduce.6.cloned.1.call-start = ((), (), s32[]{:S(2)}) async-start(), calls=%async_computation | async-start | bytes 131072 | tf_op jit(solution)/shard_map/psum | solution.py:30
  16.7 154.7 %copy-start = (f32[8,8192]{1,0:T(8,128)S(1)}, f32[8,8192]{1,0:T(8,128)}, u32[]{:S(2)}) copy-start(f32[8,8192]{1,0:T(8,128)} %param.3) | copy-start | bytes 786436
  32.5 138.9 %all-reduce.8.cloned.1.call-start = ((), (), s32[]{:S(2)}) async-start(), calls=%async_computation.1 | async-start | bytes 524288 | tf_op jit(solution)/shard_map/psum | solution.py:19
  86.4 136.2 %copy-start.1 = (f32[8,2048]{1,0:T(8,128)S(1)}, f32[8,2048]{1,0:T(8,128)}, u32[]{:S(2)}) copy-start(f32[8,2048]{1,0:T(8,128)} %all-reduce.6.cloned.1.call-done) | copy-start | bytes 196612
  104.5 118.1 %all-reduce.10.cloned.1.call-start = ((), (), s32[]{:S(2)}) async-start(), calls=%async_computation.2 | async-start | bytes 131072 | tf_op jit(solution)/shard_map/psum | solution.py:30
  191.8 135.6 %all-reduce.12.cloned.1.call-start = ((), (), s32[]{:S(2)}) async-start(), calls=%async_computation.3 | async-start | bytes 524288 | tf_op jit(solution)/shard_map/psum | solution.py:19
  222.6 111.7 %copy-start.2 = (f32[8,2048]{1,0:T(8,128)S(1)}, f32[8,2048]{1,0:T(8,128)}, u32[]{:S(2)}) copy-start(f32[8,2048]{1,0:T(8,128)} %all-reduce.10.cloned.1.call-done) | copy-start | bytes 196612
  260.4 159.0 %all-reduce.14.cloned.1.call-start = ((), (), s32[]{:S(2)}) async-start(), calls=%async_computation.4 | async-start | bytes 524288 | tf_op jit(solution)/shard_map/psum | solution.py:65
  334.4 86.7 %copy-start.3 = (f32[8,2048]{1,0:T(8,128)}, f32[8,2048]{1,0:T(8,128)S(1)}, u32[]{:S(2)}) copy-start(f32[8,2048]{1,0:T(8,128)S(1)} %multiply_add_fusion) | copy-start | bytes 196612
Sparse Core Ops, SparseCore 0:
  32.6 31.3 all-reduce.5
  104.6 66.7 all-reduce.7
  191.9 30.5 all-reduce.9
  260.6 66.7 all-reduce.11
  349.3 70.1 all-reduce.13
where the time goes:
time: 428 us
  waiting for transfers between devices  266 us (62%)
  matrix products  77.2 us (18%)
  blocking collectives  62.6 us (15%)
  between operations  13.8 us (3%)
  other arithmetic  7.47 us (2%)
    psum x2, waiting for transfers between devices, row_step(): summed = lax.psum(partial_value, 'ft')  134 us
    psum x1, waiting for transfers between devices, shards(): fitted = lax.psum(fitted, 'ft')  70.3 us
    psum x2, waiting for transfers between devices, column_step(): summed = lax.psum(partial_value, 'ex')  62.2 us
    psum x2, blocking collectives, column_step(): square = lax.psum(jnp.sum(fresh * fresh, axis=1, keepdims=True), 'ft')  42.9 us
    dot_general x2, matrix products, row_step(): lax.dot_general(right_vec.astype(jnp.bfloat16), features, (((1,), (1,)),...  33.2 us
    dot_general x2, matrix products, column_step(): jnp.dot(left_vec.astype(jnp.bfloat16), features, preferred_element_type=j...  29.3 us
    dot_general x1, matrix products, shards(): lax.dot_general(estimate.astype(jnp.bfloat16), features, (((1,), (1,)), (...  14.7 us
    psum x2, blocking collectives, row_step(): square = lax.psum(jnp.sum(fresh * fresh, axis=1, keepdims=True), 'ex')  11.3 us
  transfers between devices with their start and end apart: 5, of which 5 were waited for; matrix products, arithmetic and copies ran while one was open for 0% of the time, Pallas kernels for 0%

commit v1 on v0

v1 whole, which is shorter than its diff:
```python
import functools

import jax
import jax.numpy as jnp
from jax import lax
from jax.experimental import pallas as pl
from jax.experimental.pallas import tpu as pltpu
from jax.sharding import PartitionSpec as P

eps = 1e-06
F32 = jnp.float32
MESH = pl.DeviceIdType.MESH
NT = (((1,), (1,)), ((), ()))

BLOCKS = 4
CHUNKS = 4


def split16(x):
    hi = x.astype(jnp.bfloat16).astype(F32)
    return jnp.concatenate([hi, x - hi], axis=0).astype(jnp.bfloat16)


def fold(r):
    return r[:8] + r[8:]


def squares(x):
    return jnp.sum(x * x, axis=1, keepdims=True)


def kernel(
    n_ex, n_ft, a_ref, t_ref, est_ref, mis_ref,
    av, u16, w16, acc, pacc, rp, left, p0, p1, qs, rsb, ag, nx, nf,
    hbm, ssem, rsem,
):
    rows, cols = av.shape
    cb = cols // BLOCKS
    rc = rows // CHUNKS
    piece = rc // n_ft
    half = cols // 2
    ex, ft = lax.axis_index("ex"), lax.axis_index("ft")

    loads = []
    for j in range(BLOCKS):
        c = pl.ds(j * cb, cb)
        load = pltpu.make_async_copy(a_ref.at[:, c], av.at[:, c], hbm.at[j])
        load.start()
        loads.append(load)

    barrier = pltpu.get_barrier_semaphore()
    for axis, n, me in (("ex", n_ex, ex), ("ft", n_ft, ft)):
        @pl.loop(1, n)
        def _(d):
            pl.semaphore_signal(
                barrier, inc=1, device_id={axis: lax.rem(me + d, n)}, device_id_type=MESH
            )
    pl.semaphore_wait(barrier, n_ex + n_ft - 2)

    groups = {}

    def send(name, axis, src, dst, region):
        n, me = (n_ex, ex) if axis == "ex" else (n_ft, ft)
        g = len(groups)
        groups[name] = (g, region)

        @pl.loop(1, n)
        def _(d):
            peer = lax.rem(me + d, n)
            pltpu.make_async_remote_copy(
                src_ref=src(peer), dst_ref=dst, send_sem=ssem.at[g], recv_sem=rsem.at[g],
                device_id={axis: peer}, device_id_type=MESH,
            ).start()

    def arrive(name):
        g, region = groups[name]
        pltpu.make_async_copy(region, region, rsem.at[g]).wait()

    def put_norm(k, axis, square):
        buf, n, me = (nx, n_ex, ex) if axis == "ex" else (nf, n_ft, ft)
        buf[k, me] = jnp.broadcast_to(square, (8, 128))
        own = buf.at[k, me]
        send(("norm", axis, k), axis, lambda peer: own, own, buf.at[k, pl.ds(0, n - 1)])

    def get_norm(k, axis):
        buf, n = (nx, n_ex) if axis == "ex" else (nf, n_ft)
        arrive(("norm", axis, k))
        total = buf[k, 0]
        for i in range(1, n):
            total = total + buf[k, i]
        return jnp.sqrt(total + eps)[:, :1]

    def spread(buf, name, j, value):
        buf[j, ex] = value
        own = buf.at[j, ex]
        send((name, j), "ex", lambda peer: own, own, buf.at[j, pl.ds(0, n_ex - 1)])

    def gathered(buf, name, j):
        arrive((name, j))
        total = buf[j, 0]
        for i in range(1, n_ex):
            total = total + buf[j, i]
        return total

    def times_rows(c, first):
        @pl.loop(0, CHUNKS)
        def _(i):
            r = pl.ds(pl.multiple_of(i * rc, rc), rc)
            out = lax.dot_general(w16[:, c], av[r, c], NT, preferred_element_type=F32)
            acc[:, r] = out if first else acc[:, r] + out

    def rows_send(q, ch, c):
        r = pl.ds(ch * rc, rc)
        out = lax.dot_general(w16[:, c], av[r, c], NT, preferred_element_type=F32)
        out = fold(acc[:, r] + out)
        for i in range(n_ft):
            qs[q, ch, i] = out[:, i * piece:(i + 1) * piece]
        rsb[q, ch, ft] = qs[q, ch, ft]
        send(
            ("rs", q, ch), "ft", lambda peer: qs.at[q, ch, peer], rsb.at[q, ch, ft],
            rsb.at[q, ch, pl.ds(0, n_ft - 1)],
        )

    def rows_sum(q, ch):
        arrive(("rs", q, ch))
        total = rsb[q, ch, 0]
        for i in range(1, n_ft):
            total = total + rsb[q, ch, i]
        ag[q, ch, ft] = total
        own = ag.at[q, ch, ft]
        send(("ag", q, ch), "ft", lambda peer: own, own, ag.at[q, ch, pl.ds(0, n_ft - 1)])

    def rows_get(q, ch):
        arrive(("ag", q, ch))
        return jnp.concatenate([ag[q, ch, i] for i in range(n_ft)], axis=1)

    put_norm(0, "ex", squares(t_ref[...]))
    u16[...] = split16(t_ref[...])

    def first_columns(j):
        loads[j].wait()
        c = pl.ds(j * cb, cb)
        spread(p0, "p0", j, fold(jnp.dot(u16[...], av[:, c], preferred_element_type=F32)))

    first_columns(0)
    first_columns(1)
    beta0 = get_norm(0, "ex")
    left[...] = t_ref[...] / beta0
    square = jnp.zeros((8, 1), F32)
    for j in range(BLOCKS):
        c = pl.ds(j * cb, cb)
        fresh = gathered(p0, "p0", j) / beta0
        square = square + squares(fresh)
        rp[:, c] = fresh
        w16[:, c] = split16(fresh)
        if j == BLOCKS - 1:
            put_norm(0, "ft", square)
            break
        times_rows(c, j == 0)
        if j + 2 < BLOCKS:
            first_columns(j + 2)

    last = pl.ds((BLOCKS - 1) * cb, cb)
    for ch in range(CHUNKS):
        rows_send(0, ch, last)
        if ch >= 2:
            rows_sum(0, ch - 2)
    alpha0 = get_norm(0, "ft")

    square = jnp.zeros((8, 1), F32)
    for ch in range(CHUNKS):
        if ch + 2 < CHUNKS:
            rows_sum(0, ch + 2)
        r = pl.ds(ch * rc, rc)
        fresh = rows_get(0, ch) / alpha0 - alpha0 * left[:, r]
        square = square + squares(fresh)
        left[:, r] = fresh
        u16[:, r] = split16(fresh)
        if ch < CHUNKS - 1:
            out = jnp.dot(u16[:, r], av[r, :], preferred_element_type=F32)
            pacc[...] = out if ch == 0 else pacc[...] + out
        else:
            put_norm(1, "ex", square)
            for h in range(2):
                c = pl.ds(h * half, half)
                out = jnp.dot(u16[:, r], av[r, c], preferred_element_type=F32)
                spread(p1, "p1", h, fold(pacc[:, c] + out))
    beta1 = get_norm(1, "ex")

    square = jnp.zeros((8, 1), F32)
    for h in range(2):
        c = pl.ds(h * half, half)
        v0 = rp[:, c] / alpha0
        fresh = gathered(p1, "p1", h) / beta1 - beta1 * v0
        square = square + squares(fresh)
        rp[:, c] = v0
        est_ref[:, c] = fresh
        w16[:, c] = split16(fresh)
        if h == 0:
            times_rows(c, True)
    put_norm(1, "ft", square)
    last = pl.ds(half, half)
    for ch in range(CHUNKS):
        rows_send(1, ch, last)
        if ch >= 2:
            rows_sum(1, ch - 2)
    alpha1 = get_norm(1, "ft")
    square = jnp.zeros((8, 1), F32)
    for ch in range(CHUNKS):
        if ch + 2 < CHUNKS:
            rows_sum(1, ch + 2)
        r = pl.ds(ch * rc, rc)
        fitted = rows_get(1, ch) / alpha1
        mis_ref[:, r] = fitted
        square = square + squares(fitted - alpha1 * (left[:, r] / beta1))
    put_norm(2, "ex", square)
    beta2 = get_norm(2, "ex")

    rho = jnp.sqrt(alpha0 * alpha0 + beta1 * beta1)
    cosine = alpha0 / rho
    sine = beta1 / rho
    theta = sine * alpha1
    rho_bar = -cosine * alpha1
    step1 = cosine * beta0 / rho
    rho2 = jnp.sqrt(rho_bar * rho_bar + beta2 * beta2)
    step2 = rho_bar / rho2 * (sine * beta0) / rho2
    weight0 = step1 - step2 * (theta / rho)
    est_ref[...] = weight0 * rp[...] + step2 * (est_ref[...] / alpha1)
    scale0 = weight0 / alpha0
    for ch in range(CHUNKS):
        for i in range(n_ft):
            r = pl.ds(ch * rc + i * piece, piece)
            mis_ref[:, r] = t_ref[:, r] - (scale0 * ag[0, ch, i] + step2 * mis_ref[:, r])

    for g, region in groups.values():
        pltpu.make_async_copy(region, region, ssem.at[g]).wait()


def solution(mesh):
    n_ex, n_ft = mesh.shape["ex"], mesh.shape["ft"]

    def shards(features, targets):
        rows, cols = features.shape
        piece = rows // CHUNKS // n_ft
        n_groups = BLOCKS + 2 + 4 * CHUNKS + 5
        vmem = pltpu.VMEM
        return pl.pallas_call(
            functools.partial(kernel, n_ex, n_ft),
            out_shape=(
                jax.ShapeDtypeStruct((8, cols), F32),
                jax.ShapeDtypeStruct((8, rows), F32),
            ),
            in_specs=[pl.BlockSpec(memory_space=pl.ANY), pl.BlockSpec(memory_space=vmem)],
            out_specs=(pl.BlockSpec(memory_space=vmem), pl.BlockSpec(memory_space=vmem)),
            scratch_shapes=[
                vmem((rows, cols), jnp.bfloat16),
                vmem((16, rows), jnp.bfloat16),
                vmem((16, cols), jnp.bfloat16),
                vmem((16, rows), F32),
                vmem((16, cols), F32),
                vmem((8, cols), F32),
                vmem((8, rows), F32),
                vmem((BLOCKS, n_ex, 8, cols // BLOCKS), F32),
                vmem((2, n_ex, 8, cols // 2), F32),
                vmem((2, CHUNKS, n_ft, 8, piece), F32),
                vmem((2, CHUNKS, n_ft, 8, piece), F32),
                vmem((2, CHUNKS, n_ft, 8, piece), F32),
                vmem((3, n_ex, 8, 128), F32),
                vmem((2, n_ft, 8, 128), F32),
                pltpu.SemaphoreType.DMA((BLOCKS,)),
                pltpu.SemaphoreType.DMA((n_groups,)),
                pltpu.SemaphoreType.DMA((n_groups,)),
            ],
            compiler_params=pltpu.CompilerParams(
                collective_id=0, has_side_effects=True, vmem_limit_bytes=58 << 20
            ),
        )(features, targets)

    return jax.shard_map(
        shards,
        mesh=mesh,
        in_specs=(P("ex", "ft"), P(None, "ex")),
        out_specs=(P(None, "ft"), P(None, "ex")),
        check_vma=False,
    )
```

time: 428 us -> 72.8 us (0.17)
  waiting for transfers between devices: 266 us -> 0 us
  matrix products: 77.2 us -> 0 us
  Pallas kernels: 0 us -> 68.8 us
  blocking collectives: 62.6 us -> 0 us
  between operations: 13.8 us -> 0.64 us
  other arithmetic: 7.47 us -> 0 us
    psum x5 -> x0, waiting for transfers between devices: 266 us -> none  [the longest x2 134 us: row_step(): summed = lax.psum(partial_value, 'ft')]
    dot_general x5 -> x0, matrix products: 77.2 us -> none  [the longest x2 33.2 us: row_step(): lax.dot_general(right_vec.astype(jnp.bfloat16), features, (((1,), (1,)),...]
    pallas_call x0 -> x1, Pallas kernels: none -> 68.8 us  [shards(): pl.pallas_call(functools.partial(kernel, n_ex, n_ft), out_shape=(jax.Shap...]
    psum x5 -> x0, blocking collectives: 62.6 us -> none  [the longest x2 42.9 us: column_step(): square = lax.psum(jnp.sum(fresh * fresh, axis=1, keepdims=True), 'ft')]
    reduce_sum x5 -> x0, other arithmetic: 5.61 us -> none  [the longest x2 2.4 us: row_step(): square = lax.psum(jnp.sum(fresh * fresh, axis=1, keepdims=True), 'ex')]
  transfers between devices with their start and end apart: 5 -> 0, of which waited for: 5 -> 0; matrix products, arithmetic and copies ran while one was open for 0% -> 0% of each run, Pallas kernels for 0% -> 0%
where the time goes in v1:
time: 72.8 us; the launch traced here: 72.6 us
  Pallas kernels  68.8 us (95%)
  local copies, waits for them, and re-layouts  3.14 us (4%)
    pallas_call x1, Pallas kernels, shards(): pl.pallas_call(functools.partial(kernel, n_ex, n_ft), out_shape=(jax.Shap...  68.8 us
    unnamed x2, local copies, waits for them, and re-layouts  3.14 us

profile of v1, /device:TPU:0, one launch (start us, length us, event | category | flops | bytes accessed | tf_op | source)
XLA Modules:
  0.0 72.6 jit_solution(13501734803436364975)
XLA Ops:
  0.6 68.8 %shard_map.41 = (f32[8,2048]{1,0:T(8,128)}, f32[8,8192]{1,0:T(8,128)}) custom-call(bf16[8192,2048]{1,0:T(8,128)(2,1)} %a_ref.1, f32[8,8192]{1,0:T(8,128)} %t_ref.1), custom_call_target="tpu_custom_call" | custom-call | tf_op jit(solution)/shard_map/pallas_call | solution.py:247
  69.4 1.5 %copy.6 = f32[8,2048]{1,0:T(8,128)} copy(f32[8,2048]{1,0:T(8,128)} %get-tuple-element.4) | data formatting | bytes 131072
  70.9 1.7 %copy.7 = f32[8,8192]{1,0:T(8,128)} copy(f32[8,8192]{1,0:T(8,128)} %get-tuple-element.5) | data formatting | bytes 524288

commit v2 on v1

--- a/solution.py
+++ b/solution.py
@@ -30,8 +30,8 @@
 
 
 def kernel(
-    n_ex, n_ft, a_ref, t_ref, est_ref, mis_ref,
-    av, u16, w16, acc, pacc, rp, left, p0, p1, qs, rsb, ag, nx, nf,
+    n_ex, n_ft, n_in, a_ref, t_ref, est_ref, mis_ref,
+    av, u16, w16, acc, pacc, rp, left, p0, p1, qs, r1, s1, r2, ag, nx, nf,
     hbm, ssem, rsem,
 ):
     rows, cols = av.shape
@@ -40,6 +40,8 @@
     piece = rc // n_ft
     half = cols // 2
     ex, ft = lax.axis_index("ex"), lax.axis_index("ft")
+    n_out = n_ft // n_in
+    outer, inner = ft // n_in, lax.rem(ft, n_in)
 
     loads = []
     for j in range(BLOCKS):
@@ -60,16 +62,22 @@
     groups = {}
 
     def send(name, axis, src, dst, region):
-        n, me = (n_ex, ex) if axis == "ex" else (n_ft, ft)
+        n, me = {"ex": (n_ex, ex), "ft": (n_ft, ft), "in": (n_in, inner), "out": (n_out, outer)}[axis]
         g = len(groups)
         groups[name] = (g, region)
 
         @pl.loop(1, n)
         def _(d):
             peer = lax.rem(me + d, n)
+            device = {
+                "ex": {"ex": peer},
+                "ft": {"ft": peer},
+                "in": {"ft": outer * n_in + peer},
+                "out": {"ft": peer * n_in + inner},
+            }[axis]
             pltpu.make_async_remote_copy(
                 src_ref=src(peer), dst_ref=dst, send_sem=ssem.at[g], recv_sem=rsem.at[g],
-                device_id={axis: peer}, device_id_type=MESH,
+                device_id=device, device_id_type=MESH,
             ).start()
 
     def arrive(name):
@@ -82,13 +90,16 @@
         own = buf.at[k, me]
         send(("norm", axis, k), axis, lambda peer: own, own, buf.at[k, pl.ds(0, n - 1)])
 
-    def get_norm(k, axis):
+    def total_norm(k, axis):
         buf, n = (nx, n_ex) if axis == "ex" else (nf, n_ft)
         arrive(("norm", axis, k))
         total = buf[k, 0]
         for i in range(1, n):
             total = total + buf[k, i]
-        return jnp.sqrt(total + eps)[:, :1]
+        return total[:, :1]
+
+    def get_norm(k, axis):
+        return jnp.sqrt(total_norm(k, axis) + eps)
 
     def spread(buf, name, j, value):
         buf[j, ex] = value
@@ -102,37 +113,60 @@
             total = total + buf[j, i]
         return total
 
-    def times_rows(c, first):
-        @pl.loop(0, CHUNKS)
+    def times_rows(c, first, chunks=CHUNKS):
+        @pl.loop(0, chunks)
         def _(i):
             r = pl.ds(pl.multiple_of(i * rc, rc), rc)
             out = lax.dot_general(w16[:, c], av[r, c], NT, preferred_element_type=F32)
             acc[:, r] = out if first else acc[:, r] + out
 
-    def rows_send(q, ch, c):
+    def rows_send(q, ch, c, first):
         r = pl.ds(ch * rc, rc)
         out = lax.dot_general(w16[:, c], av[r, c], NT, preferred_element_type=F32)
-        out = fold(acc[:, r] + out)
+        out = fold(out if first else acc[:, r] + out)
         for i in range(n_ft):
-            qs[q, ch, i] = out[:, i * piece:(i + 1) * piece]
-        rsb[q, ch, ft] = qs[q, ch, ft]
+            qs[q, ch, i // n_out, i % n_out] = out[:, i * piece:(i + 1) * piece]
+        r1[q, ch, inner] = qs[q, ch, inner]
         send(
-            ("rs", q, ch), "ft", lambda peer: qs.at[q, ch, peer], rsb.at[q, ch, ft],
-            rsb.at[q, ch, pl.ds(0, n_ft - 1)],
+            ("r1", q, ch), "in", lambda peer: qs.at[q, ch, peer], r1.at[q, ch, inner],
+            r1.at[q, ch, pl.ds(0, n_in - 1)],
         )
 
-    def rows_sum(q, ch):
-        arrive(("rs", q, ch))
-        total = rsb[q, ch, 0]
-        for i in range(1, n_ft):
-            total = total + rsb[q, ch, i]
-        ag[q, ch, ft] = total
-        own = ag.at[q, ch, ft]
-        send(("ag", q, ch), "ft", lambda peer: own, own, ag.at[q, ch, pl.ds(0, n_ft - 1)])
+    def inner_sum(q, ch):
+        arrive(("r1", q, ch))
+        total = r1[q, ch, 0]
+        for i in range(1, n_in):
+            total = total + r1[q, ch, i]
+        s1[q, ch] = total
+        r2[q, ch, outer] = s1[q, ch, outer]
+        send(
+            ("r2", q, ch), "out", lambda peer: s1.at[q, ch, peer], r2.at[q, ch, outer],
+            r2.at[q, ch, pl.ds(0, n_out - 1)],
+        )
+
+    def outer_sum(q, ch):
+        arrive(("r2", q, ch))
+        total = r2[q, ch, 0]
+        for i in range(1, n_out):
+            total = total + r2[q, ch, i]
+        ag[q, ch, inner, outer] = total
+        return total
+
+    def outer_gather(q, ch):
+        own = ag.at[q, ch, inner, outer]
+        send(
+            ("g1", q, ch), "out", lambda peer: own, own,
+            ag.at[q, ch, inner, pl.ds(0, n_out - 1)],
+        )
+
+    def inner_gather(q, ch):
+        arrive(("g1", q, ch))
+        own = ag.at[q, ch, inner]
+        send(("g2", q, ch), "in", lambda peer: own, own, ag.at[q, ch, pl.ds(0, n_in - 1)])
 
     def rows_get(q, ch):
-        arrive(("ag", q, ch))
-        return jnp.concatenate([ag[q, ch, i] for i in range(n_ft)], axis=1)
+        arrive(("g2", q, ch))
+        return jnp.concatenate([ag[q, ch, i // n_out, i % n_out] for i in range(n_ft)], axis=1)
 
     put_norm(0, "ex", squares(t_ref[...]))
     u16[...] = split16(t_ref[...])
@@ -156,21 +190,32 @@
         if j == BLOCKS - 1:
             put_norm(0, "ft", square)
             break
-        times_rows(c, j == 0)
+        times_rows(c, j == 0, CHUNKS if j < BLOCKS - 2 else CHUNKS // 2)
         if j + 2 < BLOCKS:
             first_columns(j + 2)
 
-    last = pl.ds((BLOCKS - 1) * cb, cb)
     for ch in range(CHUNKS):
-        rows_send(0, ch, last)
+        late = ch >= CHUNKS // 2
+        done = (BLOCKS - 2 if late else BLOCKS - 1) * cb
+        rows_send(0, ch, pl.ds(done, cols - done), False)
+        if ch >= 1:
+            inner_sum(0, ch - 1)
         if ch >= 2:
-            rows_sum(0, ch - 2)
+            outer_sum(0, ch - 2)
+            outer_gather(0, ch - 2)
+        if ch >= 3:
+            inner_gather(0, ch - 3)
     alpha0 = get_norm(0, "ft")
 
     square = jnp.zeros((8, 1), F32)
     for ch in range(CHUNKS):
+        if ch + 3 < CHUNKS:
+            inner_sum(0, ch + 3)
         if ch + 2 < CHUNKS:
-            rows_sum(0, ch + 2)
+            outer_sum(0, ch + 2)
+            outer_gather(0, ch + 2)
+        if ch + 1 < CHUNKS:
+            inner_gather(0, ch + 1)
         r = pl.ds(ch * rc, rc)
         fresh = rows_get(0, ch) / alpha0 - alpha0 * left[:, r]
         square = square + squares(fresh)
@@ -197,23 +242,37 @@
         est_ref[:, c] = fresh
         w16[:, c] = split16(fresh)
         if h == 0:
-            times_rows(c, True)
+            times_rows(c, True, CHUNKS // 2)
     put_norm(1, "ft", square)
-    last = pl.ds(half, half)
+    def piece_square(ch, total):
+        at = ch * rc + (inner * n_out + outer) * piece
+        old = left[:, pl.ds(pl.multiple_of(at, piece), piece)]
+        return squares(total / alpha1 - alpha1 * (old / beta1))
+
+    square = jnp.zeros((8, 1), F32)
+    alpha1 = None
     for ch in range(CHUNKS):
-        rows_send(1, ch, last)
+        late = ch >= CHUNKS // 2
+        rows_send(1, ch, pl.ds(0, cols) if late else pl.ds(half, half), late)
+        if ch >= 1:
+            inner_sum(1, ch - 1)
         if ch >= 2:
-            rows_sum(1, ch - 2)
-    alpha1 = get_norm(1, "ft")
-    square = jnp.zeros((8, 1), F32)
-    for ch in range(CHUNKS):
-        if ch + 2 < CHUNKS:
-            rows_sum(1, ch + 2)
-        r = pl.ds(ch * rc, rc)
-        fitted = rows_get(1, ch) / alpha1
-        mis_ref[:, r] = fitted
-        square = square + squares(fitted - alpha1 * (left[:, r] / beta1))
-    put_norm(2, "ex", square)
+            if alpha1 is None:
+                alpha1 = get_norm(1, "ft")
+            square = square + piece_square(ch - 2, outer_sum(1, ch - 2))
+            outer_gather(1, ch - 2)
+        if ch >= 3:
+            inner_gather(1, ch - 3)
+    inner_sum(1, CHUNKS - 1)
+    square = square + piece_square(CHUNKS - 2, outer_sum(1, CHUNKS - 2))
+    outer_gather(1, CHUNKS - 2)
+    square = square + piece_square(CHUNKS - 1, outer_sum(1, CHUNKS - 1))
+    put_norm(2, "ft", square)
+    outer_gather(1, CHUNKS - 1)
+    inner_gather(1, CHUNKS - 3)
+    inner_gather(1, CHUNKS - 2)
+    put_norm(2, "ex", total_norm(2, "ft"))
+    inner_gather(1, CHUNKS - 1)
     beta2 = get_norm(2, "ex")
 
     rho = jnp.sqrt(alpha0 * alpha0 + beta1 * beta1)
@@ -227,10 +286,13 @@
     weight0 = step1 - step2 * (theta / rho)
     est_ref[...] = weight0 * rp[...] + step2 * (est_ref[...] / alpha1)
     scale0 = weight0 / alpha0
+    scale1 = step2 / alpha1
     for ch in range(CHUNKS):
+        arrive(("g2", 1, ch))
         for i in range(n_ft):
             r = pl.ds(ch * rc + i * piece, piece)
-            mis_ref[:, r] = t_ref[:, r] - (scale0 * ag[0, ch, i] + step2 * mis_ref[:, r])
+            at = (ch, i // n_out, i % n_out)
+            mis_ref[:, r] = t_ref[:, r] - (scale0 * ag[(0, *at)] + scale1 * ag[(1, *at)])
 
     for g, region in groups.values():
         pltpu.make_async_copy(region, region, ssem.at[g]).wait()
@@ -238,14 +300,15 @@
 
 def solution(mesh):
     n_ex, n_ft = mesh.shape["ex"], mesh.shape["ft"]
+    n_in = 4 if n_ft % 16 == 0 else 2
 
     def shards(features, targets):
         rows, cols = features.shape
         piece = rows // CHUNKS // n_ft
-        n_groups = BLOCKS + 2 + 4 * CHUNKS + 5
+        n_groups = BLOCKS + 2 + 8 * CHUNKS + 6
         vmem = pltpu.VMEM
         return pl.pallas_call(
-            functools.partial(kernel, n_ex, n_ft),
+            functools.partial(kernel, n_ex, n_ft, n_in),
             out_shape=(
                 jax.ShapeDtypeStruct((8, cols), F32),
                 jax.ShapeDtypeStruct((8, rows), F32),
@@ -262,11 +325,13 @@
                 vmem((8, rows), F32),
                 vmem((BLOCKS, n_ex, 8, cols // BLOCKS), F32),
                 vmem((2, n_ex, 8, cols // 2), F32),
-                vmem((2, CHUNKS, n_ft, 8, piece), F32),
-                vmem((2, CHUNKS, n_ft, 8, piece), F32),
-                vmem((2, CHUNKS, n_ft, 8, piece), F32),
+                vmem((2, CHUNKS, n_in, n_ft // n_in, 8, piece), F32),
+                vmem((2, CHUNKS, n_in, n_ft // n_in, 8, piece), F32),
+                vmem((2, CHUNKS, n_ft // n_in, 8, piece), F32),
+                vmem((2, CHUNKS, n_ft // n_in, 8, piece), F32),
+                vmem((2, CHUNKS, n_in, n_ft // n_in, 8, piece), F32),
                 vmem((3, n_ex, 8, 128), F32),
-                vmem((2, n_ft, 8, 128), F32),
+                vmem((3, n_ft, 8, 128), F32),
                 pltpu.SemaphoreType.DMA((BLOCKS,)),
                 pltpu.SemaphoreType.DMA((n_groups,)),
                 pltpu.SemaphoreType.DMA((n_groups,)),

time: 72.8 us -> 80.4 us (1.10)
  Pallas kernels: 68.8 us -> 76.4 us
    pallas_call x1, Pallas kernels: 68.8 us -> 76.4 us  [shards(): pl.pallas_call(functools.partial(kernel, n_ex, n_ft, n_in), out_shape=(ja...]
where the time goes in v2:
time: 80.4 us; the launch traced here: 80.2 us
  Pallas kernels  76.4 us (95%)
  local copies, waits for them, and re-layouts  3.14 us (4%)
    pallas_call x1, Pallas kernels, shards(): pl.pallas_call(functools.partial(kernel, n_ex, n_ft, n_in), out_shape=(ja...  76.4 us
    unnamed x2, local copies, waits for them, and re-layouts  3.14 us

profile of v2, /device:TPU:0, one launch (start us, length us, event | category | flops | bytes accessed | tf_op | source)
XLA Modules:
  0.0 80.2 jit_solution(2787902924679905259)
XLA Ops:
  0.6 76.4 %shard_map.41 = (f32[8,2048]{1,0:T(8,128)}, f32[8,8192]{1,0:T(8,128)}) custom-call(bf16[8192,2048]{1,0:T(8,128)(2,1)} %a_ref.1, f32[8,8192]{1,0:T(8,128)} %t_ref.1), custom_call_target="tpu_custom_call" | custom-call | tf_op jit(solution)/shard_map/pallas_call | solution.py:310
  77.0 1.5 %copy.6 = f32[8,2048]{1,0:T(8,128)} copy(f32[8,2048]{1,0:T(8,128)} %get-tuple-element.4) | data formatting | bytes 131072
  78.5 1.7 %copy.7 = f32[8,8192]{1,0:T(8,128)} copy(f32[8,8192]{1,0:T(8,128)} %get-tuple-element.5) | data formatting | bytes 524288

commit v3 on v1

--- a/solution.py
+++ b/solution.py
@@ -82,13 +82,16 @@
         own = buf.at[k, me]
         send(("norm", axis, k), axis, lambda peer: own, own, buf.at[k, pl.ds(0, n - 1)])
 
-    def get_norm(k, axis):
+    def total_norm(k, axis):
         buf, n = (nx, n_ex) if axis == "ex" else (nf, n_ft)
         arrive(("norm", axis, k))
         total = buf[k, 0]
         for i in range(1, n):
             total = total + buf[k, i]
-        return jnp.sqrt(total + eps)[:, :1]
+        return total[:, :1]
+
+    def get_norm(k, axis):
+        return jnp.sqrt(total_norm(k, axis) + eps)
 
     def spread(buf, name, j, value):
         buf[j, ex] = value
@@ -102,17 +105,17 @@
             total = total + buf[j, i]
         return total
 
-    def times_rows(c, first):
-        @pl.loop(0, CHUNKS)
+    def times_rows(c, first, chunks=CHUNKS):
+        @pl.loop(0, chunks)
         def _(i):
             r = pl.ds(pl.multiple_of(i * rc, rc), rc)
             out = lax.dot_general(w16[:, c], av[r, c], NT, preferred_element_type=F32)
             acc[:, r] = out if first else acc[:, r] + out
 
-    def rows_send(q, ch, c):
+    def rows_send(q, ch, c, first):
         r = pl.ds(ch * rc, rc)
         out = lax.dot_general(w16[:, c], av[r, c], NT, preferred_element_type=F32)
-        out = fold(acc[:, r] + out)
+        out = fold(out if first else acc[:, r] + out)
         for i in range(n_ft):
             qs[q, ch, i] = out[:, i * piece:(i + 1) * piece]
         rsb[q, ch, ft] = qs[q, ch, ft]
@@ -127,6 +130,9 @@
         for i in range(1, n_ft):
             total = total + rsb[q, ch, i]
         ag[q, ch, ft] = total
+        return total
+
+    def rows_gather(q, ch):
         own = ag.at[q, ch, ft]
         send(("ag", q, ch), "ft", lambda peer: own, own, ag.at[q, ch, pl.ds(0, n_ft - 1)])
 
@@ -156,21 +162,24 @@
         if j == BLOCKS - 1:
             put_norm(0, "ft", square)
             break
-        times_rows(c, j == 0)
+        times_rows(c, j == 0, CHUNKS if j < BLOCKS - 2 else CHUNKS // 2)
         if j + 2 < BLOCKS:
             first_columns(j + 2)
 
-    last = pl.ds((BLOCKS - 1) * cb, cb)
     for ch in range(CHUNKS):
-        rows_send(0, ch, last)
+        late = ch >= CHUNKS // 2
+        done = (BLOCKS - 2 if late else BLOCKS - 1) * cb
+        rows_send(0, ch, pl.ds(done, cols - done), False)
         if ch >= 2:
             rows_sum(0, ch - 2)
+            rows_gather(0, ch - 2)
     alpha0 = get_norm(0, "ft")
 
     square = jnp.zeros((8, 1), F32)
     for ch in range(CHUNKS):
         if ch + 2 < CHUNKS:
             rows_sum(0, ch + 2)
+            rows_gather(0, ch + 2)
         r = pl.ds(ch * rc, rc)
         fresh = rows_get(0, ch) / alpha0 - alpha0 * left[:, r]
         square = square + squares(fresh)
@@ -197,23 +206,29 @@
         est_ref[:, c] = fresh
         w16[:, c] = split16(fresh)
         if h == 0:
-            times_rows(c, True)
+            times_rows(c, True, CHUNKS // 2)
     put_norm(1, "ft", square)
-    last = pl.ds(half, half)
+    def piece_square(ch, total):
+        at = ch * rc + ft * piece
+        old = left[:, pl.ds(pl.multiple_of(at, piece), piece)]
+        return squares(total / alpha1 - alpha1 * (old / beta1))
+
+    square = jnp.zeros((8, 1), F32)
+    alpha1 = None
     for ch in range(CHUNKS):
-        rows_send(1, ch, last)
+        late = ch >= CHUNKS // 2
+        rows_send(1, ch, pl.ds(0, cols) if late else pl.ds(half, half), late)
         if ch >= 2:
-            rows_sum(1, ch - 2)
-    alpha1 = get_norm(1, "ft")
-    square = jnp.zeros((8, 1), F32)
-    for ch in range(CHUNKS):
-        if ch + 2 < CHUNKS:
-            rows_sum(1, ch + 2)
-        r = pl.ds(ch * rc, rc)
-        fitted = rows_get(1, ch) / alpha1
-        mis_ref[:, r] = fitted
-        square = square + squares(fitted - alpha1 * (left[:, r] / beta1))
-    put_norm(2, "ex", square)
+            if alpha1 is None:
+                alpha1 = get_norm(1, "ft")
+            square = square + piece_square(ch - 2, rows_sum(1, ch - 2))
+            rows_gather(1, ch - 2)
+    square = square + piece_square(CHUNKS - 2, rows_sum(1, CHUNKS - 2))
+    rows_gather(1, CHUNKS - 2)
+    square = square + piece_square(CHUNKS - 1, rows_sum(1, CHUNKS - 1))
+    put_norm(2, "ft", square)
+    rows_gather(1, CHUNKS - 1)
+    put_norm(2, "ex", total_norm(2, "ft"))
     beta2 = get_norm(2, "ex")
 
     rho = jnp.sqrt(alpha0 * alpha0 + beta1 * beta1)
@@ -227,10 +242,12 @@
     weight0 = step1 - step2 * (theta / rho)
     est_ref[...] = weight0 * rp[...] + step2 * (est_ref[...] / alpha1)
     scale0 = weight0 / alpha0
+    scale1 = step2 / alpha1
     for ch in range(CHUNKS):
+        arrive(("ag", 1, ch))
         for i in range(n_ft):
             r = pl.ds(ch * rc + i * piece, piece)
-            mis_ref[:, r] = t_ref[:, r] - (scale0 * ag[0, ch, i] + step2 * mis_ref[:, r])
+            mis_ref[:, r] = t_ref[:, r] - (scale0 * ag[0, ch, i] + scale1 * ag[1, ch, i])
 
     for g, region in groups.values():
         pltpu.make_async_copy(region, region, ssem.at[g]).wait()
@@ -242,7 +259,7 @@
     def shards(features, targets):
         rows, cols = features.shape
         piece = rows // CHUNKS // n_ft
-        n_groups = BLOCKS + 2 + 4 * CHUNKS + 5
+        n_groups = BLOCKS + 2 + 4 * CHUNKS + 6
         vmem = pltpu.VMEM
         return pl.pallas_call(
             functools.partial(kernel, n_ex, n_ft),
@@ -266,7 +283,7 @@
                 vmem((2, CHUNKS, n_ft, 8, piece), F32),
                 vmem((2, CHUNKS, n_ft, 8, piece), F32),
                 vmem((3, n_ex, 8, 128), F32),
-                vmem((2, n_ft, 8, 128), F32),
+                vmem((3, n_ft, 8, 128), F32),
                 pltpu.SemaphoreType.DMA((BLOCKS,)),
                 pltpu.SemaphoreType.DMA((n_groups,)),
                 pltpu.SemaphoreType.DMA((n_groups,)),

time: 72.8 us -> 70.2 us (0.964)
  Pallas kernels: 68.8 us -> 66.2 us
    pallas_call x1, Pallas kernels: 68.8 us -> 66.2 us  [shards(): pl.pallas_call(functools.partial(kernel, n_ex, n_ft), out_shape=(jax.Shap...]
where the time goes in v3:
time: 70.2 us; the launch traced here: 69.9 us
  Pallas kernels  66.2 us (94%)
  local copies, waits for them, and re-layouts  3.14 us (4%)
    pallas_call x1, Pallas kernels, shards(): pl.pallas_call(functools.partial(kernel, n_ex, n_ft), out_shape=(jax.Shap...  66.2 us
    unnamed x2, local copies, waits for them, and re-layouts  3.14 us

profile of v3, /device:TPU:0, one launch (start us, length us, event | category | flops | bytes accessed | tf_op | source)
XLA Modules:
  0.0 69.9 jit_solution(13229265286922962044)
XLA Ops:
  0.6 66.2 %shard_map.41 = (f32[8,2048]{1,0:T(8,128)}, f32[8,8192]{1,0:T(8,128)}) custom-call(bf16[8192,2048]{1,0:T(8,128)(2,1)} %a_ref.1, f32[8,8192]{1,0:T(8,128)} %t_ref.1), custom_call_target="tpu_custom_call" | custom-call | tf_op jit(solution)/shard_map/pallas_call | solution.py:264
  66.8 1.5 %copy.6 = f32[8,2048]{1,0:T(8,128)} copy(f32[8,2048]{1,0:T(8,128)} %get-tuple-element.4) | data formatting | bytes 131072
  68.3 1.7 %copy.7 = f32[8,8192]{1,0:T(8,128)} copy(f32[8,8192]{1,0:T(8,128)} %get-tuple-element.5) | data formatting | bytes 524288
